TPU v7x, 32 devices: a whole 2x2x4 slice. The times are simulated.
32 devices in a mesh: dp: 8 (over z, core), frame: 4 (over y, x).
Axes of the slice: x: 2, y: 2, z: 4, core: 2. Of those that a mesh axis runs over, the one named last changes fastest.
Arguments:
- latents: bfloat16 [8, 4, 512, 640], P('dp', 'frame'), may hold values from -6 to 6
- cotangent: bfloat16 [8, 4, 512, 640], P('dp', 'frame'), may hold values from -6 to 6
- timesteps: int32 [8], P('dp'), may hold values from 0 to 999
- spatial_weight: bfloat16 [9, 640, 640], replicated, may hold values from -0.078125 to 0.078125
- temporal_weight: bfloat16 [3, 640, 640], replicated, may hold values from -0.125 to 0.125
Outputs:
- new_spatial: float32 [9, 640, 640], P(None, 'frame')
- new_temporal: float32 [3, 640, 640], P(None, 'frame')
All inputs are finite; a program needn't handle non-finite values.
Results may differ from a plain program's by a relative error of at most 0.02.
Values may be sent and summed in bfloat16 or wider, within the bound.
A program may use at most 128 MiB of HBM per device.

v0:
```python
import math

import jax
import jax.numpy as jnp
from jax import lax
from jax.sharding import PartitionSpec as P

WIDTH = 64
SLAB = 8


def embed(timesteps, channels):
    half_width = channels // 2
    frequencies = jnp.exp(
        -math.log(10000.0) * jnp.arange(half_width, dtype=jnp.float32) / half_width
    )
    angles = timesteps.astype(jnp.float32)[:, None] * frequencies[None, :]
    return jnp.concatenate([jnp.sin(angles), jnp.cos(angles)], axis=1)


def unfold(activated, slab_rows, grid_width):
    lead_count, pixels, channels = activated.shape
    grid_cells = activated.reshape(lead_count, slab_rows, grid_width, channels)
    padded = jnp.pad(grid_cells, ((0, 0), (1, 1), (1, 1), (0, 0)))
    pieces = [
        padded[:, row_off : row_off + slab_rows, col_off : col_off + grid_width, :]
        for row_off in range(3)
        for col_off in range(3)
    ]
    return jnp.concatenate(pieces, axis=3).reshape(lead_count, pixels, 9 * channels)


def silu_slope(pre_act):
    logistic = jax.nn.sigmoid(pre_act)
    return logistic * (1.0 + pre_act * (1.0 - logistic))


def clip_factor(squares, channels):
    max_norm = 0.5 * math.sqrt(12.0) * channels
    return jnp.minimum(1.0, max_norm / (jnp.sqrt(squares) + 1e-06))


def temporal(gated_pad, cot_pad, cot_here, weight):
    frames_here = cot_here.shape[1]
    channels = cot_here.shape[3]
    cot_rows = cot_here.reshape(-1, channels)
    weight_grads = []
    grad_gated = jnp.zeros(cot_rows.shape, jnp.float32)
    for offset in range(3):
        gated_rows = gated_pad[:, offset : offset + frames_here].reshape(-1, channels)
        weight_grads.append(
            jnp.einsum("rc,rd->cd", gated_rows, cot_rows, preferred_element_type=jnp.float32)
        )
        shifted = cot_pad[:, 2 - offset : 2 - offset + frames_here].reshape(-1, channels)
        grad_gated = grad_gated + jnp.einsum(
            "rd,cd->rc", shifted, weight[offset], preferred_element_type=jnp.float32
        )
    return (jnp.stack(weight_grads), grad_gated.astype(jnp.bfloat16).reshape(cot_here.shape))


def owned_step(spatial_weight, temporal_weight, spatial_part, temporal_part, factor):
    rows_each = spatial_part.shape[1]
    cols_each = spatial_part.shape[2]
    row_start = lax.axis_index("frame") * rows_each
    spatial_here = lax.dynamic_slice(spatial_weight, (0, row_start, 0), (9, rows_each, cols_each))
    temporal_here = lax.dynamic_slice(temporal_weight, (0, row_start, 0), (3, rows_each, cols_each))
    new_spatial = spatial_here.astype(jnp.float32) - factor * spatial_part
    new_temporal = temporal_here.astype(jnp.float32) - factor * temporal_part
    return (new_spatial, new_temporal)


def on_device(latents, cotangent, timesteps, spatial_weight, temporal_weight):
    channels = latents.shape[3]
    pixels = latents.shape[2]
    shifts = embed(timesteps, channels)
    activated = jax.nn.silu(latents.astype(jnp.float32) + shifts[:, None, None, :]).astype(
        jnp.bfloat16
    )
    columns = unfold(activated.reshape(-1, pixels, channels), SLAB, WIDTH).reshape(-1, 9 * channels)
    pre_act = jnp.dot(
        columns, spatial_weight.reshape(9 * channels, channels), preferred_element_type=jnp.float32
    )
    gated = jax.nn.silu(pre_act).astype(jnp.bfloat16).reshape(latents.shape)
    pad_spec = ((0, 0), (1, 1), (0, 0), (0, 0))
    gated_rows, cot_rows = (
        lax.all_to_all(gated, "frame", split_axis=2, concat_axis=1, tiled=True),
        lax.all_to_all(cotangent, "frame", split_axis=2, concat_axis=1, tiled=True),
    )
    temporal_grad, grad_rows = temporal(
        jnp.pad(gated_rows, pad_spec), jnp.pad(cot_rows, pad_spec), cot_rows, temporal_weight
    )
    grad_gated = lax.all_to_all(grad_rows, "frame", split_axis=1, concat_axis=2, tiled=True)
    grad_pre = (
        grad_gated.reshape(pixels, channels).astype(jnp.float32) * silu_slope(pre_act)
    ).astype(jnp.bfloat16)
    spatial_grad = jnp.einsum(
        "rk,rc->kc", columns, grad_pre, preferred_element_type=jnp.float32
    ).reshape(9, channels, channels)
    spatial_part = lax.psum_scatter(
        spatial_grad.astype(jnp.bfloat16), "frame", scatter_dimension=1, tiled=True
    ).astype(jnp.float32)
    temporal_part = lax.psum_scatter(
        temporal_grad.astype(jnp.bfloat16), "frame", scatter_dimension=1, tiled=True
    ).astype(jnp.float32)
    spatial_part, temporal_part = (
        lax.psum(spatial_part.astype(jnp.bfloat16), "dp").astype(jnp.float32),
        lax.psum(temporal_part.astype(jnp.bfloat16), "dp").astype(jnp.float32),
    )
    squares = lax.psum(
        jnp.sum(spatial_part * spatial_part) + jnp.sum(temporal_part * temporal_part), "frame"
    )
    factor = clip_factor(squares, channels)
    return owned_step(spatial_weight, temporal_weight, spatial_part, temporal_part, factor)


def solution(mesh):
    in_specs = (P("dp", "frame", None, None), P("dp", "frame", None, None), P("dp"), P(), P())
    out_specs = (P(None, "frame", None), P(None, "frame", None))
    return jax.shard_map(
        on_device, mesh=mesh, in_specs=in_specs, out_specs=out_specs, check_vma=False
    )
```

profile of v0, /device:TPU:0, one launch (start us, length us, event | category | flops | bytes accessed | tf_op | source)
XLA Modules:
  0.0 300.6 jit_solution(10958119707567561780)
XLA Ops:
  7.2 2.1 copy.23
  9.3 0.5 broadcast.49
  9.8 4.5 %reduce.2 = bf16[512,640]{1,0:T(8,128)(2,1)S(1)} reduce(bf16[512,1,1,640]{3,2,1,0:T(2,128)(2,1)S(1)} %bitcast.76, bf16[]{:T(256)} %broadcast.49), dimensions={1,2}, to_apply=%bitcast.73.reduce_sub_computation | reduce | bytes 1310722
  14.3 1.0 reshape.103
  15.3 5.2 %all-to-all-start = ((bf16[4,2,40960]{2,1,0:T(2,128)(2,1)}), bf16[4,2,40960]{2,1,0:T(2,128)(2,1)S(1)}, u32[]{:S(2)}, u32[]{:S(2)}) async-start(bf16[4,2,40960]{2,1,0:T(2,128)(2,1)} %reshape.103), calls=%async_computation | async-start | bytes 1310720 | tf_op jit(solution)/shard_map/all_to_all | solution.py:87
  21.3 0.4 multiply_convert_fusion.1
  21.7 1.7 pad_slice_fusion
  23.4 1.0 constant_dynamic-update-slice_fusion.7
  24.3 1.0 constant_dynamic-update-slice_fusion.6
  25.3 0.9 constant_dynamic-update-slice_fusion.5
  26.2 1.0 constant_dynamic-update-slice_fusion.4
  27.2 1.3 bitcast_dynamic-update-slice_fusion
  28.5 1.4 all-to-all-done
  29.9 0.6 reshape.104
  30.6 0.1 copy.16
  30.6 0.1 pad_slice_fusion.10
  30.8 1.5 copy-done.1
  32.2 0.8 fusion.11
  33.0 0.8 convolution_add_fusion.1
  33.9 1.6 fusion.2
  35.5 4.2 %all-to-all-start.1 = ((bf16[1,4,128,640]{3,2,0,1:T(8,128)(2,1)}), bf16[1,4,128,640]{3,2,0,1:T(8,128)(2,1)}, u32[]{:S(2)}, u32[]{:S(2)}) async-start(bf16[1,4,128,640]{3,2,0,1:T(8,128)(2,1)} %bitcast.19), calls=%async_computation.1 | async-start | bytes 1310720 | tf_op jit(solution)/shard_map/all_to_all | solution.py:92
  39.7 0.2 reduce-scatter.5.cloned.1.call-start
  39.9 0.9 constant_dynamic-update-slice_fusion.3
  40.8 0.9 constant_dynamic-update-slice_fusion.2
  41.8 0.9 constant_dynamic-update-slice_fusion.1
  42.7 0.9 constant_dynamic-update-slice_fusion
  43.7 5.0 %all-to-all-done.1 = bf16[1,4,128,640]{3,2,0,1:T(8,128)(2,1)} async-done(((bf16[1,4,128,640]{3,2,0,1:T(8,128)(2,1)}), bf16[1,4,128,640]{3,2,0,1:T(8,128)(2,1)}, u32[]{:S(2)}, u32[]{:S(2)}) %all-to-all-start.1) | async-done | bytes 655392 | tf_op jit(solution)/shard_map/all_to_all | solution.py:92
  48.6 9.8 %fusion.22 = (bf16[1,1,512,640]{3,2,1,0:T(8,128)(2,1)S(1)}, bf16[512,640]{1,0:T(8,128)(2,1)S(1)}) fusion(bf16[1,4,128,640]{3,2,0,1:T(8,128)(2,1)} %all-to-all-done.1, bf16[512,5760]{1,0:T(8,128)(2,1)} %constant_dynamic-update-slice_fusion, bf16[5760,640]{1,0:T(8,128)(2,1)} %bitcast.94), kind=kOutput, calls=%fused_computation.50 | convolution fusion | flops 3778805760 | bytes 15237120 | tf_op jit(solution)/shard_map/dot_general | solution.py:80
  58.5 1.0 copy.22
  59.5 4.5 %reduce.3 = bf16[512,640]{1,0:T(8,128)(2,1)S(1)} reduce(bf16[512,1,1,640]{3,2,1,0:T(2,128)(2,1)S(1)} %bitcast.77, bf16[]{:T(256)} %broadcast.49), dimensions={1,2}, to_apply=%bitcast.72.reduce_sub_computation | reduce | bytes 1310722
  64.0 0.2 reshape.105
  64.2 11.3 %all_to_all.33 = bf16[4,2,40960]{2,1,0:T(2,128)(2,1)S(1)} all-to-all(bf16[4,2,40960]{2,1,0:T(2,128)(2,1)S(1)} %reshape.105), channel_id=1, replica_groups=mesh['dp'=8,'frame'=4] {'frame'}, dimensions={0} | all-to-all | bytes 1310720 | tf_op jit(solution)/shard_map/all_to_all | solution.py:86
  75.5 0.6 reshape.106
  76.2 0.7 fusion.5
  76.9 0.1 pad_slice_fusion.9
  77.1 0.7 fusion.4
  77.8 0.7 fusion.6
  78.5 1.8 pad_maximum_fusion
  80.3 8.6 %copy.12 = bf16[5760,512]{1,0:T(8,128)(2,1)} copy(bf16[5760,512]{0,1:T(8,128)(2,1)} %bitcast.11) | data formatting | bytes 11796480 | tf_op jit(solution)/shard_map/rk,rc->kc/dot_general | solution.py:96
  88.8 10.4 %convolution_convert_fusion = bf16[9,640,640]{2,1,0:T(8,128)(2,1)} fusion(bf16[9,640,512]{2,1,0:T(8,128)(2,1)} %bitcast.74, bf16[512,640]{1,0:T(8,128)(2,1)S(1)} %get-tuple-element.5), kind=kOutput, calls=%fused_computation | convolution fusion | flops 3778560000 | bytes 13926400 | tf_op jit(solution)/shard_map/rk,rc->kc/dot_general | solution.py:96
  99.3 19.0 %reduce-scatter.5.cloned.1.call-done = bf16[3,160,640]{2,1,0:T(8,128)(2,1)} async-done(((bf16[3,640,640]{2,1,0:T(8,128)(2,1)}), bf16[3,160,640]{2,1,0:T(8,128)(2,1)}) %reduce-scatter.5.cloned.1.call-update) | async-done | bytes 614416 | tf_op jit(solution)/shard_map/reduce_scatter | solution.py:102
  118.3 82.3 %reduce-scatter.3.cloned.1.call-done = bf16[9,160,640]{2,1,0:T(8,128)(2,1)} async-done(((bf16[9,640,640]{2,1,0:T(8,128)(2,1)}), bf16[9,160,640]{2,1,0:T(8,128)(2,1)}) %reduce-scatter.3.cloned.1.call-update) | async-done | bytes 1843216 | tf_op jit(solution)/shard_map/reduce_scatter | solution.py:99
  200.6 69.8 %all-reduce.6.cloned.1.call-done = (bf16[9,160,640]{2,1,0:T(8,128)(2,1)}, bf16[3,160,640]{2,1,0:T(8,128)(2,1)}) async-done(((bf16[9,160,640]{2,1,0:T(8,128)(2,1)}, bf16[3,160,640]{2,1,0:T(8,128)(2,1)}), (bf16[9,160,640]{2,1,0:T(8,128)(2,1)}, bf16[3,160,640]{2,1,0:T(8,128)(2,1)})) %all-reduce.6.cloned.1.call-update) | async-done | bytes 2457616 | tf_op jit(solution)/shard_map/psum | solution.py:106
  270.4 3.2 %fusion = f32[]{:T(128)} fusion(bf16[9,160,640]{2,1,0:T(8,128)(2,1)} %get-tuple-element.2), kind=kLoop, calls=%fused_computation.3 | loop fusion | flops 2764799 | bytes 1843204 | tf_op jit(solution)/shard_map/reduce_sum | solution.py:110
  273.6 2.0 fusion.7
  276.9 10.3 %psum.23 = f32[]{:T(128)} all-reduce(f32[]{:T(128)S(6)} %add.63), channel_id=1, replica_groups=mesh['dp'=8,'frame'=4] {'frame'}, use_global_device_ids=true, to_apply=%region_6.7 | all-reduce | flops 1 | bytes 8 | tf_op jit(solution)/shard_map/psum | solution.py:109
  288.0 2.3 fusion.8
  290.3 3.8 %fusion.1 = f32[9,160,640]{2,1,0:T(8,128)} fusion(bf16[9,160,640]{2,1,0:T(8,128)(2,1)S(1)} %copy-done, f32[]{:T(128)S(6)} %min.3, bf16[9,640,640]{2,1,0:T(8,128)(2,1)} %param.8, s32[]{:T(128)S(6)} %select_n.4), kind=kLoop, calls=%fused_computation.4 | loop fusion | flops 3686400 | bytes 7372808 | tf_op jit(solution)/shard_map/sub | solution.py:67
  (19 shorter events, 0.4 us)
Async XLA Ops:
  9.3 12.0 %copy-start.2 = (bf16[1,1,512,640]{3,2,1,0:T(8,128)(2,1)S(1)}, bf16[1,1,512,640]{3,2,1,0:T(8,128)(2,1)}, u32[]{:S(2)}) copy-start(bf16[1,1,512,640]{3,2,1,0:T(8,128)(2,1)} %param.5) | copy-start | bytes 1966084
  15.3 14.6 %all-to-all-start = ((bf16[4,2,40960]{2,1,0:T(2,128)(2,1)}), bf16[4,2,40960]{2,1,0:T(2,128)(2,1)S(1)}, u32[]{:S(2)}, u32[]{:S(2)}) async-start(bf16[4,2,40960]{2,1,0:T(2,128)(2,1)} %reshape.103), calls=%async_computation | async-start | bytes 1310720 | tf_op jit(solution)/shard_map/all_to_all | solution.py:87
  30.5 1.7 copy-start.1
  33.8 6.1 %copy-start.4 = (bf16[1,8,64,640]{3,2,1,0:T(8,128)(2,1)S(1)}, bf16[1,8,64,640]{3,2,1,0:T(8,128)(2,1)}, u32[]{:S(2)}) copy-start(bf16[1,8,64,640]{3,2,1,0:T(8,128)(2,1)} %get-tuple-element.14) | copy-start | bytes 1966084
  33.8 7.0 %copy-start.3 = (bf16[1,8,64,640]{3,2,1,0:T(8,128)(2,1)S(1)}, bf16[1,8,64,640]{3,2,1,0:T(8,128)(2,1)}, u32[]{:S(2)}) copy-start(bf16[1,8,64,640]{3,2,1,0:T(8,128)(2,1)} %get-tuple-element.15) | copy-start | bytes 1966084
  35.5 13.1 %all-to-all-start.1 = ((bf16[1,4,128,640]{3,2,0,1:T(8,128)(2,1)}), bf16[1,4,128,640]{3,2,0,1:T(8,128)(2,1)}, u32[]{:S(2)}, u32[]{:S(2)}) async-start(bf16[1,4,128,640]{3,2,0,1:T(8,128)(2,1)} %bitcast.19), calls=%async_computation.1 | async-start | bytes 1310720 | tf_op jit(solution)/shard_map/all_to_all | solution.py:92
  39.7 78.7 %reduce-scatter.5.cloned.1.call-start = ((), (), s32[]{:S(2)}) async-start(), calls=%async_computation.6 | async-start | bytes 3072000 | tf_op jit(solution)/shard_map/reduce_scatter | solution.py:102
  80.2 120.4 %reduce-scatter.3.cloned.1.call-start = ((), (), s32[]{:S(2)}) async-start(), calls=%async_computation.5 | async-start | bytes 9216000 | tf_op jit(solution)/shard_map/reduce_scatter | solution.py:99
  99.3 171.1 %all-reduce.6.cloned.1.call-start = ((), (), s32[]{:S(2)}) async-start(), calls=%async_computation.7 | async-start | bytes 4915200 | tf_op jit(solution)/shard_map/psum | solution.py:106
  270.4 17.6 %copy-start.5 = (bf16[3,160,640]{2,1,0:T(8,128)(2,1)S(1)}, bf16[3,160,640]{2,1,0:T(8,128)(2,1)}, u32[]{:S(2)}) copy-start(bf16[3,160,640]{2,1,0:T(8,128)(2,1)} %get-tuple-element.3) | copy-start | bytes 1843204
  270.4 19.9 %copy-start = (bf16[9,160,640]{2,1,0:T(8,128)(2,1)S(1)}, bf16[9,160,640]{2,1,0:T(8,128)(2,1)}, u32[]{:S(2)}) copy-start(bf16[9,160,640]{2,1,0:T(8,128)(2,1)} %get-tuple-element.2) | copy-start | bytes 5529604
Sparse Core Ops, SparseCore 0:
  80.4 37.9 reduce-scatter.4
  121.3 79.2 reduce-scatter.2
  203.1 67.2 all-reduce.5
where the time goes:
time: 301 us
  waiting for transfers between devices  177 us (59%)
  local copies, waits for them, and re-layouts  25.7 us (9%)
  matrix products  25.5 us (8%)
  other arithmetic  24 us (8%)
  blocking collectives  21.7 us (7%)
  between operations  16.6 us (6%)
  starting transfers between devices  9.64 us (3%)
    reduce_scatter x1, waiting for transfers between devices, on_device(): lax.psum_scatter(spatial_grad.astype(jnp.bfloat16), 'frame', scatter_dime...  82.3 us
    psum x1, waiting for transfers between devices, on_device(): lax.psum(spatial_part.astype(jnp.bfloat16), 'dp').astype(jnp.float32)  69.8 us
    reduce_scatter x1, waiting for transfers between devices, on_device(): lax.psum_scatter(temporal_grad.astype(jnp.bfloat16), 'frame', scatter_dim...  19 us
    unnamed x27, local copies, waits for them, and re-layouts  13.4 us
    all_to_all x1, blocking collectives, on_device(): lax.all_to_all(gated, 'frame', split_axis=2, concat_axis=1, tiled=True)  11.3 us
    dot_general x1, matrix products, on_device(): jnp.einsum('rk,rc->kc', columns, grad_pre, preferred_element_type=jnp.flo...  10.4 us
    psum x1, blocking collectives, on_device(): lax.psum(jnp.sum(spatial_part * spatial_part) + jnp.sum(temporal_part * t...  10.3 us
    unnamed x3, other arithmetic  10.3 us
  transfers between devices with their start and end apart: 5, of which 5 were waited for; matrix products, arithmetic and copies ran while one was open for 10% of the time, Pallas kernels for 0%

commit v1 on v0

v1 whole, which is shorter than its diff:
```python
import math

import jax
import jax.numpy as jnp
from jax import lax
from jax.sharding import PartitionSpec as P

WIDTH = 64
SLAB = 8


def embed(timesteps, channels):
    half_width = channels // 2
    frequencies = jnp.exp(
        -math.log(10000.0) * jnp.arange(half_width, dtype=jnp.float32) / half_width
    )
    angles = timesteps.astype(jnp.float32)[:, None] * frequencies[None, :]
    return jnp.concatenate([jnp.sin(angles), jnp.cos(angles)], axis=1)


def unfold(activated, slab_rows, grid_width):
    lead_count, pixels, channels = activated.shape
    grid_cells = activated.reshape(lead_count, slab_rows, grid_width, channels)
    padded = jnp.pad(grid_cells, ((0, 0), (1, 1), (1, 1), (0, 0)))
    pieces = [
        padded[:, row_off : row_off + slab_rows, col_off : col_off + grid_width, :]
        for row_off in range(3)
        for col_off in range(3)
    ]
    return jnp.concatenate(pieces, axis=3).reshape(lead_count, pixels, 9 * channels)


def silu_slope(pre_act):
    logistic = jax.nn.sigmoid(pre_act)
    return logistic * (1.0 + pre_act * (1.0 - logistic))


def clip_factor(squares, channels):
    max_norm = 0.5 * math.sqrt(12.0) * channels
    return jnp.minimum(1.0, max_norm / (jnp.sqrt(squares) + 1e-06))


def exchange(array, axis_name, mask):
    count = lax.axis_size(axis_name)
    return lax.ppermute(array, axis_name, [(i, i ^ mask) for i in range(count)])


def halve(array, dim, axis_name, mask):
    mine = jnp.bitwise_and(lax.axis_index(axis_name) // mask, 1)
    keep = lax.dynamic_index_in_dim(array, mine, dim, keepdims=False)
    send = lax.dynamic_index_in_dim(array, 1 - mine, dim, keepdims=False)
    got = exchange(send, axis_name, mask)
    return (keep.astype(jnp.float32) + got.astype(jnp.float32)).astype(jnp.bfloat16)


def masks_of(axis_name):
    count = lax.axis_size(axis_name)
    return [1 << bit for bit in range(count.bit_length() - 1)]


def share_of(grads, high_first):
    taps, channels, width = grads.shape
    owners = lax.axis_size("frame")
    rows = channels // owners
    part = grads.astype(jnp.bfloat16).reshape(taps, owners, rows, width)
    part = jnp.swapaxes(part, 0, 1).reshape(owners, taps * rows, width)
    dp_masks = masks_of("dp")
    spare = -(taps * rows) % lax.axis_size("dp")
    if spare:
        part = jnp.pad(part, ((0, 0), (0, spare), (0, 0)))
    lead = part.shape[0]
    part = halve(part.reshape(lead, 2, -1, width), 1, "dp", dp_masks[0])
    frame_masks = masks_of("frame")
    for mask in reversed(frame_masks) if high_first else frame_masks:
        lead = part.shape[0] // 2
        if high_first:
            part = halve(part.reshape((2, lead) + part.shape[1:]), 0, "frame", mask)
        else:
            part = halve(part.reshape((lead, 2) + part.shape[1:]), 1, "frame", mask)
    part = part[0]
    for mask in dp_masks[1:]:
        part = halve(part.reshape(2, -1, width), 0, "dp", mask)
    return part


def whole_of(part, taps, rows):
    for mask in reversed(masks_of("dp")):
        got = exchange(part, "dp", mask)
        upper = jnp.bitwise_and(lax.axis_index("dp") // mask, 1) == 1
        part = jnp.concatenate([jnp.where(upper, got, part), jnp.where(upper, part, got)], axis=0)
    return part[: taps * rows].reshape(taps, rows, -1).astype(jnp.float32)


def owned_step(spatial_weight, temporal_weight, spatial_part, temporal_part, factor):
    rows_each = spatial_part.shape[1]
    cols_each = spatial_part.shape[2]
    row_start = lax.axis_index("frame") * rows_each
    spatial_here = lax.dynamic_slice(spatial_weight, (0, row_start, 0), (9, rows_each, cols_each))
    temporal_here = lax.dynamic_slice(temporal_weight, (0, row_start, 0), (3, rows_each, cols_each))
    new_spatial = spatial_here.astype(jnp.float32) - factor * spatial_part
    new_temporal = temporal_here.astype(jnp.float32) - factor * temporal_part
    return (new_spatial, new_temporal)


def on_device(latents, cotangent, timesteps, spatial_weight, temporal_weight):
    channels = latents.shape[3]
    pixels = latents.shape[2]
    frames = lax.axis_size("frame")
    cot_here = cotangent.reshape(pixels, channels)
    cot_next = lax.ppermute(cot_here, "frame", [(i, i - 1) for i in range(1, frames)])
    cot_prev = lax.ppermute(cot_here, "frame", [(i, i + 1) for i in range(frames - 1)])
    shifts = embed(timesteps, channels)
    activated = jax.nn.silu(latents.astype(jnp.float32) + shifts[:, None, None, :]).astype(
        jnp.bfloat16
    )
    columns = unfold(activated.reshape(-1, pixels, channels), SLAB, WIDTH).reshape(-1, 9 * channels)
    pre_act = jnp.dot(
        columns, spatial_weight.reshape(9 * channels, channels), preferred_element_type=jnp.float32
    )
    gated = jax.nn.silu(pre_act).astype(jnp.bfloat16)
    shifted = (cot_next, cot_here, cot_prev)
    grad_gated = jnp.zeros((pixels, channels), jnp.float32)
    for offset in range(3):
        grad_gated = grad_gated + jnp.einsum(
            "rd,cd->rc", shifted[offset], temporal_weight[offset], preferred_element_type=jnp.float32
        )
    grad_pre = (
        grad_gated.astype(jnp.bfloat16).astype(jnp.float32) * silu_slope(pre_act)
    ).astype(jnp.bfloat16)
    temporal_grad = jnp.stack(
        [
            jnp.einsum("rc,rd->cd", gated, cot, preferred_element_type=jnp.float32)
            for cot in shifted
        ]
    )
    shares = [share_of(temporal_grad, False)]
    for row_off in range(3):
        block = columns[:, 3 * row_off * channels : 3 * (row_off + 1) * channels]
        grads = jnp.einsum("rk,rc->kc", block, grad_pre, preferred_element_type=jnp.float32)
        shares.append(share_of(grads.reshape(3, channels, channels), row_off % 2 == 0))
    local = sum(jnp.sum(jnp.square(share.astype(jnp.float32))) for share in shares)
    squares = lax.psum(local, ("dp", "frame"))
    temporal_part, *spatial_parts = [whole_of(share, 3, channels // frames) for share in shares]
    spatial_part = jnp.concatenate(spatial_parts, axis=0)
    factor = clip_factor(squares, channels)
    return owned_step(spatial_weight, temporal_weight, spatial_part, temporal_part, factor)


def solution(mesh):
    in_specs = (P("dp", "frame", None, None), P("dp", "frame", None, None), P("dp"), P(), P())
    out_specs = (P(None, "frame", None), P(None, "frame", None))
    return jax.shard_map(
        on_device, mesh=mesh, in_specs=in_specs, out_specs=out_specs, check_vma=False
    )
```

time: 301 us -> 192 us (0.64)
  waiting for transfers between devices: 177 us -> 49.9 us
  starting transfers between devices: 9.64 us -> 47.1 us
  blocking collectives: 21.7 us -> 38 us
  local copies, waits for them, and re-layouts: 25.7 us -> 10.7 us
  between operations: 16.6 us -> 5.38 us
  other arithmetic: 24 us -> 16.1 us
    reduce_scatter x2 -> x0, waiting for transfers between devices: 101 us -> none  [the longest x1 82.3 us: on_device(): lax.psum_scatter(spatial_grad.astype(jnp.bfloat16), 'frame', scatter_dime...]
    psum x1 -> x0, waiting for transfers between devices: 69.8 us -> none  [on_device(): lax.psum(spatial_part.astype(jnp.bfloat16), 'dp').astype(jnp.float32)]
    ppermute x0 -> x34, waiting for transfers between devices: none -> 49.9 us  [the longest x32 49.9 us: exchange(): return lax.ppermute(array, axis_name, [(i, i ^ mask) for i in range(count)])]
    ppermute x0 -> x34, starting transfers between devices: none -> 47.1 us  [the longest x32 39.5 us: exchange(): return lax.ppermute(array, axis_name, [(i, i ^ mask) for i in range(count)])]
    psum x1, blocking collectives: 10.3 us -> 38 us  [on_device(): squares = lax.psum(local, ('dp', 'frame'))]
    all_to_all x1 -> x0, blocking collectives: 11.3 us -> none  [on_device(): lax.all_to_all(gated, 'frame', split_axis=2, concat_axis=1, tiled=True)]
    unnamed x3 -> x2, other arithmetic: 10.3 us -> 0.42 us
    all_to_all x2 -> x0, starting transfers between devices: 9.34 us -> none  [the longest x1 5.16 us: on_device(): lax.all_to_all(cotangent, 'frame', split_axis=2, concat_axis=1, tiled=True)]
  transfers between devices with their start and end apart: 5 -> 34, of which waited for: 5 -> 15; matrix products, arithmetic and copies ran while one was open for 10% -> 21% of each run, Pallas kernels for 0% -> 0%
where the time goes in v1:
time: 192 us
  waiting for transfers between devices  49.9 us (26%)
  starting transfers between devices  47.1 us (25%)
  blocking collectives  38 us (20%)
  matrix products  24.4 us (13%)
  other arithmetic  16.1 us (8%)
  local copies, waits for them, and re-layouts  10.7 us (6%)
  between operations  5.38 us (3%)
    ppermute x32, waiting for transfers between devices, exchange(): return lax.ppermute(array, axis_name, [(i, i ^ mask) for i in range(count)])  49.9 us
    ppermute x32, starting transfers between devices, exchange(): return lax.ppermute(array, axis_name, [(i, i ^ mask) for i in range(count)])  39.5 us
    psum x1, blocking collectives, on_device(): squares = lax.psum(local, ('dp', 'frame'))  38 us
    dot_general x3, matrix products, on_device(): jnp.einsum('rc,rd->cd', gated, cot, preferred_element_type=jnp.float32)  6.61 us
    ppermute x1, starting transfers between devices, on_device(): lax.ppermute(cot_here, 'frame', [(i, i + 1) for i in range(frames - 1)])  6.33 us
    dot_general x3, matrix products, on_device(): jnp.einsum('rd,cd->rc', shifted[offset], temporal_weight[offset], preferr...  6.31 us
    dot_general x1, matrix products, on_device(): jnp.dot(columns, spatial_weight.reshape(9 * channels, channels), preferre...  6.07 us
    unnamed x37, local copies, waits for them, and re-layouts  5.91 us
  transfers between devices with their start and end apart: 34, of which 15 were waited for; matrix products, arithmetic and copies ran while one was open for 21% of the time, Pallas kernels for 0%

profile of v1, /device:TPU:0, one launch (start us, length us, event | category | flops | bytes accessed | tf_op | source)
XLA Modules:
  0.0 191.7 jit_solution(9020935094205153781)
XLA Ops:
  0.6 1.3 collective-permute-start
  1.9 6.3 %collective-permute-start.1 = (bf16[512,640]{1,0:T(8,128)(2,1)}, bf16[512,640]{1,0:T(8,128)(2,1)}, u32[]{:S(2)}, u32[]{:S(2)}) collective-permute-start(bf16[512,640]{1,0:T(8,128)(2,1)} %bitcast.221), channel_id=1, source_target_pairs={{0,1},{1,2},{2,3},{4,5},{5,6},{6,7},{8,9},{9,10},{10,11},{12,13},{... | collective-permute-start | bytes 1966088 | tf_op jit(solution)/shard_map/ppermute | solution.py:111
  9.1 1.5 multiply_convert_fusion.1
  12.6 0.9 copy-done
  15.1 6.1 %fusion.27 = (bf16[640,512]{0,1:T(8,128)(2,1)}, f32[512,640]{1,0:T(8,128)}) fusion(bf16[512,5760]{1,0:T(8,128)(2,1)S(1)} %constant_dynamic-update-slice_fusion, bf16[5760,640]{1,0:T(8,128)(2,1)S(1)} %bitcast.224), kind=kOutput, calls=%fused_computation.45 | convolution fusion | flops 3776512000 | bytes 15237120 | tf_op jit(solution)/shard_map/dot_general | solution.py:117
  21.2 2.2 %copy.8 = bf16[640,512]{1,0:T(8,128)(2,1)} copy(bf16[640,512]{0,1:T(8,128)(2,1)} %get-tuple-element.42) | data formatting | bytes 1310720 | tf_op jit(solution)/shard_map/convert_element_type | solution.py:120
  23.3 2.8 %fusion.28 = bf16[1,4,160,640]{3,2,1,0:T(8,128)(2,1)} fusion(bf16[4,160,512]{2,1,0:T(8,128)(2,1)} %bitcast.219, bf16[1,1,512,640]{3,2,1,0:T(8,128)(2,1)} %param.6), kind=kOutput, calls=%fused_computation.46 | convolution fusion | flops 419840000 | bytes 2129920 | tf_op jit(solution)/shard_map/rc,rd->cd/dot_general | solution.py:132
  26.2 1.2 fusion.70
  27.4 2.2 %fusion.35 = f32[512,640]{1,0:T(8,128)S(1)} fusion(bf16[3,640,640]{2,1,0:T(8,128)(2,1)} %param.9, bf16[1,1,512,640]{3,2,1,0:T(8,128)(2,1)} %param.6), kind=kOutput, calls=%fused_computation.71 | convolution fusion | flops 419430400 | bytes 2785280 | tf_op jit(solution)/shard_map/rd,cd->rc/dot_general | solution.py:124
  29.7 1.8 convolution_convert_fusion.5
  31.6 1.9 convolution_convert_fusion.3
  34.2 1.5 copy-done.9
  35.7 1.9 fusion.33
  37.6 2.2 %fusion.23 = bf16[512,640]{1,0:T(8,128)(2,1)S(1)} fusion(f32[512,640]{1,0:T(8,128)S(1)} %fusion.33, f32[512,640]{1,0:T(8,128)S(1)} %fusion.35, bf16[512,640]{1,0:T(8,128)(2,1)} %collective-permute-done, f32[512,640]{1,0:T(8,128)S(1)} %copy-done.12, bf16[3,640,640]{2,1,0:T(8,128)(2,1)S(1)} %copy-done.9), kind=kOutput, calls=%fused_computation.36 | convolution fusion | flops 423690240 | bytes 6062080 | tf_op jit(solution)/shard_map/rd,cd->rc/dot_general | solution.py:124
  39.9 2.0 %convolution_convert_fusion.2 = bf16[1920,640]{1,0:T(8,128)(2,1)S(1)} fusion(bf16[512,640]{1,0:T(8,128)(2,1)S(1)} %fusion.23, bf16[512,640]{1,0:T(8,128)(2,1)S(1)} %bitcast.199, bf16[512,640]{1,0:T(8,128)(2,1)S(1)} %bitcast.197, bf16[512,640]{1,0:T(8,128)(2,1)S(1)} %bitcast.201), kind=kOutput, calls=%fused_computation.3 | convolution fusion | flops 1265418240 | bytes 5079040 | tf_op jit(solution)/shard_map/rk,rc->kc/dot_general | solution.py:139
  43.4 1.7 convolution_convert_fusion.1
  45.5 1.7 convolution_convert_fusion
  48.6 2.6 %collective-permute-start.3 = (bf16[2,240,640]{2,1,0:T(8,128)(2,1)S(1)}, bf16[2,240,640]{2,1,0:T(8,128)(2,1)S(1)}, u32[]{:S(2)}, u32[]{:S(2)}) collective-permute-start(bf16[2,240,640]{2,1,0:T(8,128)(2,1)S(1)} %dynamic-slice_bitcast_fusion.7), channel_id=1, source_target_pairs={{0,1},{1,0},{2,3},{3,2},{4,5},{5,4},{6,7},{7,6},{8,9},{9,8},{10,11... | collective-permute-start | bytes 1843208 | tf_op jit(solution)/shard_map/ppermute | solution.py:45
  51.6 3.7 %collective-permute-start.8 = (bf16[2,240,640]{2,1,0:T(8,128)(2,1)S(1)}, bf16[2,240,640]{2,1,0:T(8,128)(2,1)S(1)}, u32[]{:S(2)}, u32[]{:S(2)}) collective-permute-start(bf16[2,240,640]{2,1,0:T(8,128)(2,1)S(1)} %dynamic-slice_bitcast_fusion.6), channel_id=1, source_target_pairs={{0,2},{1,3},{2,0},{3,1},{4,6},{5,7},{6,4},{7,5},{8,10},{9,11},{10,... | collective-permute-start | bytes 1843208 | tf_op jit(solution)/shard_map/ppermute | solution.py:45
  56.6 9.3 %collective-permute-done.3 = bf16[2,240,640]{2,1,0:T(8,128)(2,1)S(1)} collective-permute-done((bf16[2,240,640]{2,1,0:T(8,128)(2,1)S(1)}, bf16[2,240,640]{2,1,0:T(8,128)(2,1)S(1)}, u32[]{:S(2)}, u32[]{:S(2)}) %collective-permute-start.3) | collective-permute-done | bytes 614432 | tf_op jit(solution)/shard_map/ppermute | solution.py:45
  66.0 4.0 %collective-permute-start.4 = (bf16[1,240,640]{2,1,0:T(8,128)(2,1)S(1)}, bf16[1,240,640]{2,1,0:T(8,128)(2,1)S(1)}, u32[]{:S(2)}, u32[]{:S(2)}) collective-permute-start(bf16[1,240,640]{2,1,0:T(8,128)(2,1)S(1)} %constant_dynamic-slice_fusion.3), channel_id=1, source_target_pairs={{0,2},{1,3},{2,0},{3,1},{4,6},{5,7},{6,4},{7,5},{8,10},{9,11},{10,... | collective-permute-start | bytes 921608 | tf_op jit(solution)/shard_map/ppermute | solution.py:45
  70.3 1.8 collective-permute-start.9
  72.1 6.9 %collective-permute-done.13 = bf16[2,240,640]{2,1,0:T(8,128)(2,1)S(1)} collective-permute-done((bf16[2,240,640]{2,1,0:T(8,128)(2,1)S(1)}, bf16[2,240,640]{2,1,0:T(8,128)(2,1)S(1)}, u32[]{:S(2)}, u32[]{:S(2)}) %collective-permute-start.13) | collective-permute-done | bytes 614432 | tf_op jit(solution)/shard_map/ppermute | solution.py:45
  79.2 4.0 %collective-permute-start.14 = (bf16[1,240,640]{2,1,0:T(8,128)(2,1)S(1)}, bf16[1,240,640]{2,1,0:T(8,128)(2,1)S(1)}, u32[]{:S(2)}, u32[]{:S(2)}) collective-permute-start(bf16[1,240,640]{2,1,0:T(8,128)(2,1)S(1)} %constant_dynamic-slice_fusion.1), channel_id=1, source_target_pairs={{0,2},{1,3},{2,0},{3,1},{4,6},{5,7},{6,4},{7,5},{8,10},{9,11},{10,... | collective-permute-start | bytes 921608 | tf_op jit(solution)/shard_map/ppermute | solution.py:45
  83.4 1.8 collective-permute-start.19
  85.2 4.5 %collective-permute-done.4 = bf16[1,240,640]{2,1,0:T(8,128)(2,1)S(1)} collective-permute-done((bf16[1,240,640]{2,1,0:T(8,128)(2,1)S(1)}, bf16[1,240,640]{2,1,0:T(8,128)(2,1)S(1)}, u32[]{:S(2)}, u32[]{:S(2)}) %collective-permute-start.4) | collective-permute-done | bytes 307232 | tf_op jit(solution)/shard_map/ppermute | solution.py:45
  89.8 1.7 collective-permute-start.5
  92.1 3.2 %collective-permute-done.14 = bf16[1,240,640]{2,1,0:T(8,128)(2,1)S(1)} collective-permute-done((bf16[1,240,640]{2,1,0:T(8,128)(2,1)S(1)}, bf16[1,240,640]{2,1,0:T(8,128)(2,1)S(1)}, u32[]{:S(2)}, u32[]{:S(2)}) %collective-permute-start.14) | collective-permute-done | bytes 307232 | tf_op jit(solution)/shard_map/ppermute | solution.py:45
  95.5 1.7 collective-permute-start.15
  97.9 2.7 %collective-permute-start.6 = (bf16[60,640]{1,0:T(8,128)(2,1)S(1)}, bf16[60,640]{1,0:T(8,128)(2,1)S(1)}, u32[]{:S(2)}, u32[]{:S(2)}) collective-permute-start(bf16[60,640]{1,0:T(8,128)(2,1)S(1)} %dynamic-slice_bitcast_fusion.15), channel_id=1, source_target_pairs={{0,16},{4,20},{8,24},{12,28},{16,0},{20,4},{24,8},{28,12},{1,17},{... | collective-permute-start | bytes 230408 | tf_op jit(solution)/shard_map/ppermute | solution.py:45
  101.0 4.2 %collective-permute-done.15 = bf16[120,640]{1,0:T(8,128)(2,1)S(1)} collective-permute-done((bf16[120,640]{1,0:T(8,128)(2,1)S(1)}, bf16[120,640]{1,0:T(8,128)(2,1)S(1)}, u32[]{:S(2)}, u32[]{:S(2)}) %collective-permute-start.15) | collective-permute-done | bytes 153632 | tf_op jit(solution)/shard_map/ppermute | solution.py:45
  105.4 1.9 collective-permute-start.16
  107.3 1.0 collective-permute-done.20
  109.8 2.2 %collective-permute-start.31 = (bf16[60,640]{1,0:T(8,128)(2,1)S(1)}, bf16[60,640]{1,0:T(8,128)(2,1)S(1)}, u32[]{:S(2)}, u32[]{:S(2)}) collective-permute-start(bf16[60,640]{1,0:T(8,128)(2,1)S(1)} %get-tuple-element.9), channel_id=1, source_target_pairs={{0,16},{4,20},{8,24},{12,28},{16,0},{20,4},{24,8},{28,12},{1,17},{... | collective-permute-start | bytes 230408 | tf_op jit(solution)/shard_map/ppermute | solution.py:45
  112.7 2.9 %collective-permute-done.16 = bf16[60,640]{1,0:T(8,128)(2,1)S(1)} collective-permute-done((bf16[60,640]{1,0:T(8,128)(2,1)S(1)}, bf16[60,640]{1,0:T(8,128)(2,1)S(1)}, u32[]{:S(2)}, u32[]{:S(2)}) %collective-permute-start.16) | collective-permute-done | bytes 76832 | tf_op jit(solution)/shard_map/ppermute | solution.py:45
  116.3 2.0 %collective-permute-done.21 = bf16[60,640]{1,0:T(8,128)(2,1)S(1)} collective-permute-done((bf16[60,640]{1,0:T(8,128)(2,1)S(1)}, bf16[60,640]{1,0:T(8,128)(2,1)S(1)}, u32[]{:S(2)}, u32[]{:S(2)}) %collective-permute-start.21) | collective-permute-done | bytes 76832 | tf_op jit(solution)/shard_map/ppermute | solution.py:45
  121.3 38.0 %psum.7 = f32[]{:T(128)} all-reduce(f32[]{:T(128)S(6)} %add.230), channel_id=1, replica_groups=mesh['dp'=8,'frame'=4] {'dp','frame'}, use_global_device_ids=true, to_apply=%region_4.5 | all-reduce | flops 1 | bytes 8 | tf_op jit(solution)/shard_map/psum | solution.py:142
  160.0 3.0 %collective-permute-start.22 = (bf16[60,640]{1,0:T(8,128)(2,1)S(1)}, bf16[60,640]{1,0:T(8,128)(2,1)S(1)}, u32[]{:S(2)}, u32[]{:S(2)}) collective-permute-start(bf16[60,640]{1,0:T(8,128)(2,1)S(1)} %get-tuple-element.7), channel_id=1, source_target_pairs={{0,16},{4,20},{8,24},{12,28},{16,0},{20,4},{24,8},{28,12},{1,17},{... | collective-permute-start | bytes 230408 | tf_op jit(solution)/shard_map/ppermute | solution.py:45
  163.1 2.8 %collective-permute-start.28 = (bf16[60,640]{1,0:T(8,128)(2,1)S(1)}, bf16[60,640]{1,0:T(8,128)(2,1)S(1)}, u32[]{:S(2)}, u32[]{:S(2)}) collective-permute-start(bf16[60,640]{1,0:T(8,128)(2,1)S(1)} %get-tuple-element.3), channel_id=1, source_target_pairs={{0,16},{4,20},{8,24},{12,28},{16,0},{20,4},{24,8},{28,12},{1,17},{... | collective-permute-start | bytes 230408 | tf_op jit(solution)/shard_map/ppermute | solution.py:45
  166.2 5.2 %collective-permute-done.22 = bf16[60,640]{1,0:T(8,128)(2,1)S(1)} collective-permute-done((bf16[60,640]{1,0:T(8,128)(2,1)S(1)}, bf16[60,640]{1,0:T(8,128)(2,1)S(1)}, u32[]{:S(2)}, u32[]{:S(2)}) %collective-permute-start.22) | collective-permute-done | bytes 76832 | tf_op jit(solution)/shard_map/ppermute | solution.py:45
  171.6 1.6 collective-permute-done.25
  174.2 1.3 collective-permute-start.29
  175.5 1.3 collective-permute-done.32
  177.0 3.1 %collective-permute-done.23 = bf16[120,640]{1,0:T(8,128)(2,1)S(1)} collective-permute-done((bf16[120,640]{1,0:T(8,128)(2,1)S(1)}, bf16[120,640]{1,0:T(8,128)(2,1)S(1)}, u32[]{:S(2)}, u32[]{:S(2)}) %collective-permute-start.23) | collective-permute-done | bytes 153632 | tf_op jit(solution)/shard_map/ppermute | solution.py:45
  180.3 2.7 %collective-permute-done.26 = bf16[120,640]{1,0:T(8,128)(2,1)S(1)} collective-permute-done((bf16[120,640]{1,0:T(8,128)(2,1)S(1)}, bf16[120,640]{1,0:T(8,128)(2,1)S(1)}, u32[]{:S(2)}, u32[]{:S(2)}) %collective-permute-start.26) | collective-permute-done | bytes 153632 | tf_op jit(solution)/shard_map/ppermute | solution.py:45
  183.1 1.5 collective-permute-done.29
  185.4 2.2 %convert_subtract_fusion = f32[3,160,640]{2,1,0:T(8,128)} fusion(f32[3,160,640]{2,1,0:T(8,128)S(1)} %bitcast.177, bf16[3,640,640]{2,1,0:T(8,128)(2,1)} %param.9, s32[]{:T(128)S(6)} %select_n.219), kind=kLoop, calls=%fused_computation.56 | loop fusion | flops 614400 | bytes 3072004 | tf_op jit(solution)/shard_map/sub | solution.py:101
  187.8 3.9 %multiply_subtract_fusion = f32[9,160,640]{2,1,0:T(8,128)} fusion(bf16[3,160,640]{2,1,0:T(8,128)(2,1)S(1)} %bitcast.208, bf16[3,160,640]{2,1,0:T(8,128)(2,1)S(1)} %bitcast.207, bf16[3,160,640]{2,1,0:T(8,128)(2,1)S(1)} %bitcast.206, f32[]{:T(128)S(6)} %min.3, bf16[9,640,640]{2,1,0:T(8,128)(2,1)} %param.8, s32[]{:T(128)S(6)} %select_n.219), kind=kLoop, calls=%fused_computation | loop fusion | flops 8294400 | bytes 7372808 | tf_op jit(solution)/shard_map/sub | solution.py:100
  (152 shorter events, 18.4 us)
Async XLA Ops:
  0.6 29.0 %collective-permute-start = (bf16[512,640]{1,0:T(8,128)(2,1)}, bf16[512,640]{1,0:T(8,128)(2,1)}, u32[]{:S(2)}, u32[]{:S(2)}) collective-permute-start(bf16[512,640]{1,0:T(8,128)(2,1)} %bitcast.220), channel_id=1, source_target_pairs={{1,0},{2,1},{3,2},{5,4},{6,5},{7,6},{9,8},{10,9},{11,10},{13,12},{... | collective-permute-start | bytes 1966088 | tf_op jit(solution)/shard_map/ppermute | solution.py:110
  1.9 29.6 %collective-permute-start.1 = (bf16[512,640]{1,0:T(8,128)(2,1)}, bf16[512,640]{1,0:T(8,128)(2,1)}, u32[]{:S(2)}, u32[]{:S(2)}) collective-permute-start(bf16[512,640]{1,0:T(8,128)(2,1)} %bitcast.221), channel_id=1, source_target_pairs={{0,1},{1,2},{2,3},{4,5},{5,6},{6,7},{8,9},{9,10},{10,11},{12,13},{... | collective-permute-start | bytes 1966088 | tf_op jit(solution)/shard_map/ppermute | solution.py:111
  10.6 3.9 %slice-start = ((s8[7372800]{0:T(1024)(128)(4,1)}), s8[3178496]{0:T(1024)(128)(4,1)S(1)}, s32[]{:S(2)}) async-start(s8[7372800]{0:T(1024)(128)(4,1)} %bitcast.222), calls=%async_computation | async-start | bytes 6356992
  11.1 1.1 copy-start.7
  11.2 1.3 copy-start.5
  11.2 2.8 %copy-start.1 = (bf16[1,8,64,640]{3,2,1,0:T(8,128)(2,1)}, bf16[1,8,64,640]{3,2,1,0:T(8,128)(2,1)S(1)}, u32[]{:S(2)}) copy-start(bf16[1,8,64,640]{3,2,1,0:T(8,128)(2,1)S(1)} %get-tuple-element.14) | copy-start | bytes 1966084
  12.4 1.1 copy-start
  12.4 2.7 %slice-start.1 = ((s8[7372800]{0:T(1024)(128)(4,1)}), s8[4194304]{0:T(1024)(128)(4,1)S(1)}, s32[]{:S(2)}) async-start(s8[7372800]{0:T(1024)(128)(4,1)} %bitcast.222), calls=%async_computation.1 | async-start | bytes 8388608
  27.4 2.3 %copy-start.12 = (f32[512,640]{1,0:T(8,128)S(1)}, f32[512,640]{1,0:T(8,128)}, u32[]{:S(2)}) copy-start(f32[512,640]{1,0:T(8,128)} %get-tuple-element.43) | copy-start | bytes 3932164
  31.5 1.9 %copy-start.10 = (bf16[1,4,160,640]{3,2,1,0:T(8,128)(2,1)S(1)}, bf16[1,4,160,640]{3,2,1,0:T(8,128)(2,1)}, u32[]{:S(2)}) copy-start(bf16[1,4,160,640]{3,2,1,0:T(8,128)(2,1)} %fusion.28) | copy-start | bytes 2457604
  34.0 1.7 copy-start.9
  34.2 14.0 %collective-permute-start.2 = (bf16[4,240,640]{2,1,0:T(8,128)(2,1)S(1)}, bf16[4,240,640]{2,1,0:T(8,128)(2,1)S(1)}, u32[]{:S(2)}, u32[]{:S(2)}) collective-permute-start(bf16[4,240,640]{2,1,0:T(8,128)(2,1)S(1)} %dynamic-slice_bitcast_fusion.3), channel_id=1, source_target_pairs={{0,4},{4,0},{8,12},{12,8},{16,20},{20,16},{24,28},{28,24},{1,5},{5... | collective-permute-start | bytes 3686408 | tf_op jit(solution)/shard_map/ppermute | solution.py:45
  37.6 2.2 %copy-start.4 = (bf16[1,8,64,640]{3,2,1,0:T(8,128)(2,1)S(1)}, bf16[1,8,64,640]{3,2,1,0:T(8,128)(2,1)}, u32[]{:S(2)}) copy-start(bf16[1,8,64,640]{3,2,1,0:T(8,128)(2,1)} %copy-done.3) | copy-start | bytes 1966084
  37.6 2.2 %copy-start.6 = (bf16[1,8,64,640]{3,2,1,0:T(8,128)(2,1)S(1)}, bf16[1,8,64,640]{3,2,1,0:T(8,128)(2,1)}, u32[]{:S(2)}) copy-start(bf16[1,8,64,640]{3,2,1,0:T(8,128)(2,1)} %copy-done.5) | copy-start | bytes 1966084
  37.6 2.2 %copy-start.8 = (bf16[1,8,64,640]{3,2,1,0:T(8,128)(2,1)S(1)}, bf16[1,8,64,640]{3,2,1,0:T(8,128)(2,1)}, u32[]{:S(2)}) copy-start(bf16[1,8,64,640]{3,2,1,0:T(8,128)(2,1)} %copy-done.7) | copy-start | bytes 1966084
  42.1 1.1 copy-start.2
  42.1 1.3 copy-start.11
  42.2 8.9 %collective-permute-start.7 = (bf16[4,240,640]{2,1,0:T(8,128)(2,1)S(1)}, bf16[4,240,640]{2,1,0:T(8,128)(2,1)S(1)}, u32[]{:S(2)}, u32[]{:S(2)}) collective-permute-start(bf16[4,240,640]{2,1,0:T(8,128)(2,1)S(1)} %dynamic-slice_bitcast_fusion.2), channel_id=1, source_target_pairs={{0,4},{4,0},{8,12},{12,8},{16,20},{20,16},{24,28},{28,24},{1,5},{5... | collective-permute-start | bytes 3686408 | tf_op jit(solution)/shard_map/ppermute | solution.py:45
  45.5 9.8 %collective-permute-start.12 = (bf16[4,240,640]{2,1,0:T(8,128)(2,1)S(1)}, bf16[4,240,640]{2,1,0:T(8,128)(2,1)S(1)}, u32[]{:S(2)}, u32[]{:S(2)}) collective-permute-start(bf16[4,240,640]{2,1,0:T(8,128)(2,1)S(1)} %dynamic-slice_bitcast_fusion.1), channel_id=1, source_target_pairs={{0,4},{4,0},{8,12},{12,8},{16,20},{20,16},{24,28},{28,24},{1,5},{5... | collective-permute-start | bytes 3686408 | tf_op jit(solution)/shard_map/ppermute | solution.py:45
  47.6 8.4 %collective-permute-start.17 = (bf16[4,240,640]{2,1,0:T(8,128)(2,1)S(1)}, bf16[4,240,640]{2,1,0:T(8,128)(2,1)S(1)}, u32[]{:S(2)}, u32[]{:S(2)}) collective-permute-start(bf16[4,240,640]{2,1,0:T(8,128)(2,1)S(1)} %dynamic-slice_bitcast_fusion), channel_id=1, source_target_pairs={{0,4},{4,0},{8,12},{12,8},{16,20},{20,16},{24,28},{28,24},{1,5},{5... | collective-permute-start | bytes 3686408 | tf_op jit(solution)/shard_map/ppermute | solution.py:45
  48.6 17.2 %collective-permute-start.3 = (bf16[2,240,640]{2,1,0:T(8,128)(2,1)S(1)}, bf16[2,240,640]{2,1,0:T(8,128)(2,1)S(1)}, u32[]{:S(2)}, u32[]{:S(2)}) collective-permute-start(bf16[2,240,640]{2,1,0:T(8,128)(2,1)S(1)} %dynamic-slice_bitcast_fusion.7), channel_id=1, source_target_pairs={{0,1},{1,0},{2,3},{3,2},{4,5},{5,4},{6,7},{7,6},{8,9},{9,8},{10,11... | collective-permute-start | bytes 1843208 | tf_op jit(solution)/shard_map/ppermute | solution.py:45
  51.6 18.5 %collective-permute-start.8 = (bf16[2,240,640]{2,1,0:T(8,128)(2,1)S(1)}, bf16[2,240,640]{2,1,0:T(8,128)(2,1)S(1)}, u32[]{:S(2)}, u32[]{:S(2)}) collective-permute-start(bf16[2,240,640]{2,1,0:T(8,128)(2,1)S(1)} %dynamic-slice_bitcast_fusion.6), channel_id=1, source_target_pairs={{0,2},{1,3},{2,0},{3,1},{4,6},{5,7},{6,4},{7,5},{8,10},{9,11},{10,... | collective-permute-start | bytes 1843208 | tf_op jit(solution)/shard_map/ppermute | solution.py:45
  55.7 23.3 %collective-permute-start.13 = (bf16[2,240,640]{2,1,0:T(8,128)(2,1)S(1)}, bf16[2,240,640]{2,1,0:T(8,128)(2,1)S(1)}, u32[]{:S(2)}, u32[]{:S(2)}) collective-permute-start(bf16[2,240,640]{2,1,0:T(8,128)(2,1)S(1)} %dynamic-slice_bitcast_fusion.5), channel_id=1, source_target_pairs={{0,1},{1,0},{2,3},{3,2},{4,5},{5,4},{6,7},{7,6},{8,9},{9,8},{10,11... | collective-permute-start | bytes 1843208 | tf_op jit(solution)/shard_map/ppermute | solution.py:45
  56.5 26.8 %collective-permute-start.18 = (bf16[2,240,640]{2,1,0:T(8,128)(2,1)S(1)}, bf16[2,240,640]{2,1,0:T(8,128)(2,1)S(1)}, u32[]{:S(2)}, u32[]{:S(2)}) collective-permute-start(bf16[2,240,640]{2,1,0:T(8,128)(2,1)S(1)} %dynamic-slice_bitcast_fusion.4), channel_id=1, source_target_pairs={{0,2},{1,3},{2,0},{3,1},{4,6},{5,7},{6,4},{7,5},{8,10},{9,11},{10,... | collective-permute-start | bytes 1843208 | tf_op jit(solution)/shard_map/ppermute | solution.py:45
  66.0 23.7 %collective-permute-start.4 = (bf16[1,240,640]{2,1,0:T(8,128)(2,1)S(1)}, bf16[1,240,640]{2,1,0:T(8,128)(2,1)S(1)}, u32[]{:S(2)}, u32[]{:S(2)}) collective-permute-start(bf16[1,240,640]{2,1,0:T(8,128)(2,1)S(1)} %constant_dynamic-slice_fusion.3), channel_id=1, source_target_pairs={{0,2},{1,3},{2,0},{3,1},{4,6},{5,7},{6,4},{7,5},{8,10},{9,11},{10,... | collective-permute-start | bytes 921608 | tf_op jit(solution)/shard_map/ppermute | solution.py:45
  70.3 21.2 %collective-permute-start.9 = (bf16[1,240,640]{2,1,0:T(8,128)(2,1)S(1)}, bf16[1,240,640]{2,1,0:T(8,128)(2,1)S(1)}, u32[]{:S(2)}, u32[]{:S(2)}) collective-permute-start(bf16[1,240,640]{2,1,0:T(8,128)(2,1)S(1)} %constant_dynamic-slice_fusion.2), channel_id=1, source_target_pairs={{0,1},{1,0},{2,3},{3,2},{4,5},{5,4},{6,7},{7,6},{8,9},{9,8},{10,11... | collective-permute-start | bytes 921608 | tf_op jit(solution)/shard_map/ppermute | solution.py:45
  79.2 16.2 %collective-permute-start.14 = (bf16[1,240,640]{2,1,0:T(8,128)(2,1)S(1)}, bf16[1,240,640]{2,1,0:T(8,128)(2,1)S(1)}, u32[]{:S(2)}, u32[]{:S(2)}) collective-permute-start(bf16[1,240,640]{2,1,0:T(8,128)(2,1)S(1)} %constant_dynamic-slice_fusion.1), channel_id=1, source_target_pairs={{0,2},{1,3},{2,0},{3,1},{4,6},{5,7},{6,4},{7,5},{8,10},{9,11},{10,... | collective-permute-start | bytes 921608 | tf_op jit(solution)/shard_map/ppermute | solution.py:45
  83.4 13.7 %collective-permute-start.19 = (bf16[1,240,640]{2,1,0:T(8,128)(2,1)S(1)}, bf16[1,240,640]{2,1,0:T(8,128)(2,1)S(1)}, u32[]{:S(2)}, u32[]{:S(2)}) collective-permute-start(bf16[1,240,640]{2,1,0:T(8,128)(2,1)S(1)} %constant_dynamic-slice_fusion), channel_id=1, source_target_pairs={{0,1},{1,0},{2,3},{3,2},{4,5},{5,4},{6,7},{7,6},{8,9},{9,8},{10,11... | collective-permute-start | bytes 921608 | tf_op jit(solution)/shard_map/ppermute | solution.py:45
  89.8 7.9 %collective-permute-start.5 = (bf16[120,640]{1,0:T(8,128)(2,1)S(1)}, bf16[120,640]{1,0:T(8,128)(2,1)S(1)}, u32[]{:S(2)}, u32[]{:S(2)}) collective-permute-start(bf16[120,640]{1,0:T(8,128)(2,1)S(1)} %dynamic-slice_bitcast_fusion.11), channel_id=1, source_target_pairs={{0,8},{4,12},{8,0},{12,4},{16,24},{20,28},{24,16},{28,20},{1,9},{5... | collective-permute-start | bytes 460808 | tf_op jit(solution)/shard_map/ppermute | solution.py:45
  91.6 8.9 %collective-permute-start.10 = (bf16[120,640]{1,0:T(8,128)(2,1)S(1)}, bf16[120,640]{1,0:T(8,128)(2,1)S(1)}, u32[]{:S(2)}, u32[]{:S(2)}) collective-permute-start(bf16[120,640]{1,0:T(8,128)(2,1)S(1)} %dynamic-slice_bitcast_fusion.10), channel_id=1, source_target_pairs={{0,8},{4,12},{8,0},{12,4},{16,24},{20,28},{24,16},{28,20},{1,9},{5... | collective-permute-start | bytes 460808 | tf_op jit(solution)/shard_map/ppermute | solution.py:45
  95.5 9.8 %collective-permute-start.15 = (bf16[120,640]{1,0:T(8,128)(2,1)S(1)}, bf16[120,640]{1,0:T(8,128)(2,1)S(1)}, u32[]{:S(2)}, u32[]{:S(2)}) collective-permute-start(bf16[120,640]{1,0:T(8,128)(2,1)S(1)} %dynamic-slice_bitcast_fusion.9), channel_id=1, source_target_pairs={{0,8},{4,12},{8,0},{12,4},{16,24},{20,28},{24,16},{28,20},{1,9},{5... | collective-permute-start | bytes 460808 | tf_op jit(solution)/shard_map/ppermute | solution.py:45
  97.2 11.0 %collective-permute-start.20 = (bf16[120,640]{1,0:T(8,128)(2,1)S(1)}, bf16[120,640]{1,0:T(8,128)(2,1)S(1)}, u32[]{:S(2)}, u32[]{:S(2)}) collective-permute-start(bf16[120,640]{1,0:T(8,128)(2,1)S(1)} %dynamic-slice_bitcast_fusion.8), channel_id=1, source_target_pairs={{0,8},{4,12},{8,0},{12,4},{16,24},{20,28},{24,16},{28,20},{1,9},{5... | collective-permute-start | bytes 460808 | tf_op jit(solution)/shard_map/ppermute | solution.py:45
  97.9 11.3 %collective-permute-start.6 = (bf16[60,640]{1,0:T(8,128)(2,1)S(1)}, bf16[60,640]{1,0:T(8,128)(2,1)S(1)}, u32[]{:S(2)}, u32[]{:S(2)}) collective-permute-start(bf16[60,640]{1,0:T(8,128)(2,1)S(1)} %dynamic-slice_bitcast_fusion.15), channel_id=1, source_target_pairs={{0,16},{4,20},{8,24},{12,28},{16,0},{20,4},{24,8},{28,12},{1,17},{... | collective-permute-start | bytes 230408 | tf_op jit(solution)/shard_map/ppermute | solution.py:45
  100.6 11.3 %collective-permute-start.11 = (bf16[60,640]{1,0:T(8,128)(2,1)S(1)}, bf16[60,640]{1,0:T(8,128)(2,1)S(1)}, u32[]{:S(2)}, u32[]{:S(2)}) collective-permute-start(bf16[60,640]{1,0:T(8,128)(2,1)S(1)} %dynamic-slice_bitcast_fusion.14), channel_id=1, source_target_pairs={{0,16},{4,20},{8,24},{12,28},{16,0},{20,4},{24,8},{28,12},{1,17},{... | collective-permute-start | bytes 230408 | tf_op jit(solution)/shard_map/ppermute | solution.py:45
  105.4 10.2 %collective-permute-start.16 = (bf16[60,640]{1,0:T(8,128)(2,1)S(1)}, bf16[60,640]{1,0:T(8,128)(2,1)S(1)}, u32[]{:S(2)}, u32[]{:S(2)}) collective-permute-start(bf16[60,640]{1,0:T(8,128)(2,1)S(1)} %dynamic-slice_bitcast_fusion.13), channel_id=1, source_target_pairs={{0,16},{4,20},{8,24},{12,28},{16,0},{20,4},{24,8},{28,12},{1,17},{... | collective-permute-start | bytes 230408 | tf_op jit(solution)/shard_map/ppermute | solution.py:45
  108.3 9.9 %collective-permute-start.21 = (bf16[60,640]{1,0:T(8,128)(2,1)S(1)}, bf16[60,640]{1,0:T(8,128)(2,1)S(1)}, u32[]{:S(2)}, u32[]{:S(2)}) collective-permute-start(bf16[60,640]{1,0:T(8,128)(2,1)S(1)} %dynamic-slice_bitcast_fusion.12), channel_id=1, source_target_pairs={{0,16},{4,20},{8,24},{12,28},{16,0},{20,4},{24,8},{28,12},{1,17},{... | collective-permute-start | bytes 230408 | tf_op jit(solution)/shard_map/ppermute | solution.py:45
  109.8 56.3 %collective-permute-start.31 = (bf16[60,640]{1,0:T(8,128)(2,1)S(1)}, bf16[60,640]{1,0:T(8,128)(2,1)S(1)}, u32[]{:S(2)}, u32[]{:S(2)}) collective-permute-start(bf16[60,640]{1,0:T(8,128)(2,1)S(1)} %get-tuple-element.9), channel_id=1, source_target_pairs={{0,16},{4,20},{8,24},{12,28},{16,0},{20,4},{24,8},{28,12},{1,17},{... | collective-permute-start | bytes 230408 | tf_op jit(solution)/shard_map/ppermute | solution.py:45
  160.0 11.4 %collective-permute-start.22 = (bf16[60,640]{1,0:T(8,128)(2,1)S(1)}, bf16[60,640]{1,0:T(8,128)(2,1)S(1)}, u32[]{:S(2)}, u32[]{:S(2)}) collective-permute-start(bf16[60,640]{1,0:T(8,128)(2,1)S(1)} %get-tuple-element.7), channel_id=1, source_target_pairs={{0,16},{4,20},{8,24},{12,28},{16,0},{20,4},{24,8},{28,12},{1,17},{... | collective-permute-start | bytes 230408 | tf_op jit(solution)/shard_map/ppermute | solution.py:45
  163.1 10.1 %collective-permute-start.25 = (bf16[60,640]{1,0:T(8,128)(2,1)S(1)}, bf16[60,640]{1,0:T(8,128)(2,1)S(1)}, u32[]{:S(2)}, u32[]{:S(2)}) collective-permute-start(bf16[60,640]{1,0:T(8,128)(2,1)S(1)} %get-tuple-element.5), channel_id=1, source_target_pairs={{0,16},{4,20},{8,24},{12,28},{16,0},{20,4},{24,8},{28,12},{1,17},{... | collective-permute-start | bytes 230408 | tf_op jit(solution)/shard_map/ppermute | solution.py:45
  163.1 11.0 %collective-permute-start.28 = (bf16[60,640]{1,0:T(8,128)(2,1)S(1)}, bf16[60,640]{1,0:T(8,128)(2,1)S(1)}, u32[]{:S(2)}, u32[]{:S(2)}) collective-permute-start(bf16[60,640]{1,0:T(8,128)(2,1)S(1)} %get-tuple-element.3), channel_id=1, source_target_pairs={{0,16},{4,20},{8,24},{12,28},{16,0},{20,4},{24,8},{28,12},{1,17},{... | collective-permute-start | bytes 230408 | tf_op jit(solution)/shard_map/ppermute | solution.py:45
  166.1 10.7 %collective-permute-start.32 = (bf16[120,640]{1,0:T(8,128)(2,1)S(1)}, bf16[120,640]{1,0:T(8,128)(2,1)S(1)}, u32[]{:S(2)}, u32[]{:S(2)}) collective-permute-start(bf16[120,640]{1,0:T(8,128)(2,1)S(1)} %pad_maximum_fusion.10), channel_id=1, source_target_pairs={{0,8},{4,12},{8,0},{12,4},{16,24},{20,28},{24,16},{28,20},{1,9},{5... | collective-permute-start | bytes 460808 | tf_op jit(solution)/shard_map/ppermute | solution.py:45
  171.5 8.6 %collective-permute-start.23 = (bf16[120,640]{1,0:T(8,128)(2,1)S(1)}, bf16[120,640]{1,0:T(8,128)(2,1)S(1)}, u32[]{:S(2)}, u32[]{:S(2)}) collective-permute-start(bf16[120,640]{1,0:T(8,128)(2,1)S(1)} %pad_maximum_fusion.7), channel_id=1, source_target_pairs={{0,8},{4,12},{8,0},{12,4},{16,24},{20,28},{24,16},{28,20},{1,9},{5... | collective-permute-start | bytes 460808 | tf_op jit(solution)/shard_map/ppermute | solution.py:45
  173.2 9.7 %collective-permute-start.26 = (bf16[120,640]{1,0:T(8,128)(2,1)S(1)}, bf16[120,640]{1,0:T(8,128)(2,1)S(1)}, u32[]{:S(2)}, u32[]{:S(2)}) collective-permute-start(bf16[120,640]{1,0:T(8,128)(2,1)S(1)} %pad_maximum_fusion.8), channel_id=1, source_target_pairs={{0,8},{4,12},{8,0},{12,4},{16,24},{20,28},{24,16},{28,20},{1,9},{5... | collective-permute-start | bytes 460808 | tf_op jit(solution)/shard_map/ppermute | solution.py:45
  174.2 10.4 %collective-permute-start.29 = (bf16[120,640]{1,0:T(8,128)(2,1)S(1)}, bf16[120,640]{1,0:T(8,128)(2,1)S(1)}, u32[]{:S(2)}, u32[]{:S(2)}) collective-permute-start(bf16[120,640]{1,0:T(8,128)(2,1)S(1)} %pad_maximum_fusion.9), channel_id=1, source_target_pairs={{0,8},{4,12},{8,0},{12,4},{16,24},{20,28},{24,16},{28,20},{1,9},{5... | collective-permute-start | bytes 460808 | tf_op jit(solution)/shard_map/ppermute | solution.py:45
  176.9 7.9 %collective-permute-start.33 = (bf16[240,640]{1,0:T(8,128)(2,1)S(1)}, bf16[240,640]{1,0:T(8,128)(2,1)S(1)}, u32[]{:S(2)}, u32[]{:S(2)}) collective-permute-start(bf16[240,640]{1,0:T(8,128)(2,1)S(1)} %pad_maximum_fusion.6), channel_id=1, source_target_pairs={{0,4},{4,0},{8,12},{12,8},{16,20},{20,16},{24,28},{28,24},{1,5},{5... | collective-permute-start | bytes 921608 | tf_op jit(solution)/shard_map/ppermute | solution.py:45
  180.2 4.7 %collective-permute-start.24 = (bf16[240,640]{1,0:T(8,128)(2,1)S(1)}, bf16[240,640]{1,0:T(8,128)(2,1)S(1)}, u32[]{:S(2)}, u32[]{:S(2)}) collective-permute-start(bf16[240,640]{1,0:T(8,128)(2,1)S(1)} %pad_maximum_fusion.3), channel_id=1, source_target_pairs={{0,4},{4,0},{8,12},{12,8},{16,20},{20,16},{24,28},{28,24},{1,5},{5... | collective-permute-start | bytes 921608 | tf_op jit(solution)/shard_map/ppermute | solution.py:45
  183.1 2.1 %collective-permute-start.27 = (bf16[240,640]{1,0:T(8,128)(2,1)S(1)}, bf16[240,640]{1,0:T(8,128)(2,1)S(1)}, u32[]{:S(2)}, u32[]{:S(2)}) collective-permute-start(bf16[240,640]{1,0:T(8,128)(2,1)S(1)} %pad_maximum_fusion.4), channel_id=1, source_target_pairs={{0,4},{4,0},{8,12},{12,8},{16,20},{20,16},{24,28},{28,24},{1,5},{5... | collective-permute-start | bytes 921608 | tf_op jit(solution)/shard_map/ppermute | solution.py:45
  184.7 2.9 %collective-permute-start.30 = (bf16[240,640]{1,0:T(8,128)(2,1)S(1)}, bf16[240,640]{1,0:T(8,128)(2,1)S(1)}, u32[]{:S(2)}, u32[]{:S(2)}) collective-permute-start(bf16[240,640]{1,0:T(8,128)(2,1)S(1)} %pad_maximum_fusion.5), channel_id=1, source_target_pairs={{0,4},{4,0},{8,12},{12,8},{16,20},{20,16},{24,28},{28,24},{1,5},{5... | collective-permute-start | bytes 921608 | tf_op jit(solution)/shard_map/ppermute | solution.py:45
  (1 other events, 0.8 us)
